TPU v7x, 128 devices: a whole 4x4x4 slice. The times are simulated.
128 devices in a mesh: dp: 2 (over core), ctx: 16 (over y, x), tp: 4 (over z).
Axes of the slice: x: 4, y: 4, z: 4, core: 2. Of those that a mesh axis runs over, the one named last changes fastest.
Arguments:
- queries: bfloat16 [4, 8192, 6144], P('dp', 'tp', 'ctx'), may hold values from -6 to 6
- key_proj: bfloat16 [4, 8192, 6144], P('dp', 'tp', 'ctx'), may hold values from -6 to 6
- value_proj: bfloat16 [4, 8192, 6144], P('dp', 'tp', 'ctx'), may hold values from -6 to 6
- grad_output: bfloat16 [4, 8192, 6144], P('dp', 'tp', 'ctx'), may hold values from -6 to 6
- filters: float32 [512, 128], P('tp'), may hold values from -0.5 to 0.5
- group_of: int32 [8192], P('tp'), may hold values from 0 to 511, as said below
Outputs:
- gated_out: bfloat16 [4, 8192, 6144], P('dp', 'tp', 'ctx')
- grad_queries: bfloat16 [4, 8192, 6144], P('dp', 'tp', 'ctx')
- grad_keys: bfloat16 [4, 8192, 6144], P('dp', 'tp', 'ctx')
- grad_values: bfloat16 [4, 8192, 6144], P('dp', 'tp', 'ctx')
- grad_filters: float32 [512, 128], P('tp')
Inputs may be any that keep to these rules, and one draw needn't show every extreme that they name: `group_of`: channels come in aligned runs of 16 consecutive channels that share one filter row, and every filter row serves exactly one run.
All inputs are finite; a program needn't handle non-finite values.
Results may differ from a plain program's by a relative error of at most 0.0058.
Values may be sent and summed in bfloat16 or wider, within the bound.
A program may use at most 192 MiB of HBM per device.

v0:
```python
import jax
import jax.numpy as jnp
from jax import lax
from jax.sharding import PartitionSpec as P

D = 8192
GROUPS = 512


def passed_along(block, axis, distance):
    devices = range(lax.axis_size(axis))
    route = [(i - distance, i) for i in devices if i - distance in devices]
    return lax.ppermute(block, axis, route)


def band_apply(matrix, rows_in, block_rows, groups_here):
    channels, positions = rows_in.shape
    blocked = rows_in.reshape(
        groups_here, channels // groups_here, positions // block_rows, block_rows
    )
    result = jnp.einsum("rmbj,rij->rmbi", blocked, matrix, preferred_element_type=jnp.float32)
    return result.reshape(channels, positions)


def band_adjoint(matrix, rows_in, block_rows, groups_here):
    channels, positions = rows_in.shape
    blocked = rows_in.reshape(
        groups_here, channels // groups_here, positions // block_rows, block_rows
    )
    result = jnp.einsum("rmbj,rji->rmbi", blocked, matrix, preferred_element_type=jnp.float32)
    return result.reshape(channels, positions)


def band_outer(left_rows, right_rows, block_rows, groups_here):
    channels, positions = left_rows.shape
    shape_four = (groups_here, channels // groups_here, positions // block_rows, block_rows)
    return jnp.einsum(
        "rmbi,rmbj->rij",
        left_rows.reshape(shape_four),
        right_rows.reshape(shape_four),
        preferred_element_type=jnp.float32,
    )


def shards(queries, key_proj, value_proj, grad_output, filters, group_of):
    wide = jnp.float32
    windows, channels, positions = queries.shape
    block_rows = filters.shape[1]
    members = D // GROUPS
    groups_here = channels // members
    filter_table = lax.all_gather(filters.astype(jnp.bfloat16), "tp", axis=0, tiled=True)
    run_group = group_of.reshape(groups_here, members)[:, 0]
    selector = (run_group[:, None] == jnp.arange(GROUPS, dtype=jnp.int32)[None, :]).astype(
        jnp.bfloat16
    )
    run_filters = jnp.dot(selector, filter_table, preferred_element_type=wide).astype(jnp.bfloat16)
    template = jnp.concatenate(
        [
            jnp.zeros((groups_here, 1), jnp.bfloat16),
            run_filters[:, ::-1],
            jnp.zeros((groups_here, block_rows), jnp.bfloat16),
        ],
        axis=1,
    )
    toeplitz = jnp.tile(template, (1, block_rows))[:, : 2 * block_rows * block_rows]
    toeplitz = toeplitz.reshape(groups_here, block_rows, 2 * block_rows)
    lower_band = toeplitz[:, :, :block_rows]
    upper_band = toeplitz[:, :, block_rows:]
    product = (key_proj.astype(wide) * value_proj.astype(wide)).astype(jnp.bfloat16)
    key_rim, value_rim = passed_along(
        (key_proj[:, :, -block_rows:], value_proj[:, :, -block_rows:]), "ctx", 1
    )
    before = (key_rim.astype(wide) * value_rim.astype(wide)).astype(jnp.bfloat16)
    backward = (grad_output.astype(wide) * queries.astype(wide)).astype(jnp.bfloat16)
    after = passed_along(backward[:, :, :block_rows], "ctx", -1)
    gated_list = []
    gradq_list = []
    gradk_list = []
    gradv_list = []
    outer_total = jnp.zeros((groups_here, block_rows, 2 * block_rows), wide)
    for window in range(windows):
        product_w = product[window]
        backward_w = backward[window]
        previous = jnp.concatenate([before[window], product_w[:, :-block_rows]], axis=1)
        following = jnp.concatenate([backward_w[:, block_rows:], after[window]], axis=1)
        mixed_rows = band_apply(upper_band, product_w, block_rows, groups_here)
        mixed_rows = mixed_rows + band_apply(lower_band, previous, block_rows, groups_here)
        gated_list.append((queries[window].astype(wide) * mixed_rows).astype(jnp.bfloat16))
        gradq_list.append((grad_output[window].astype(wide) * mixed_rows).astype(jnp.bfloat16))
        upward = band_adjoint(upper_band, backward_w, block_rows, groups_here)
        upward = upward + band_adjoint(lower_band, following, block_rows, groups_here)
        gradk_list.append((upward * value_proj[window].astype(wide)).astype(jnp.bfloat16))
        gradv_list.append((upward * key_proj[window].astype(wide)).astype(jnp.bfloat16))
        outer_total = outer_total + jnp.concatenate(
            [
                band_outer(backward_w, previous, block_rows, groups_here),
                band_outer(backward_w, product_w, block_rows, groups_here),
            ],
            axis=2,
        )
    gated_out = jnp.stack(gated_list, axis=0)
    grad_queries = jnp.stack(gradq_list, axis=0)
    grad_keys = jnp.stack(gradk_list, axis=0)
    grad_values = jnp.stack(gradv_list, axis=0)
    flattened = outer_total.reshape(groups_here, 2 * block_rows * block_rows)
    flattened = jnp.pad(flattened, ((0, 0), (0, block_rows)))
    diagonals = jnp.sum(flattened.reshape(groups_here, block_rows, 2 * block_rows + 1), axis=1)
    run_grad = diagonals[:, block_rows:0:-1]
    scale_by = 1.0 / (windows * positions * lax.axis_size("dp") * lax.axis_size("ctx"))
    table_grad = (
        jnp.dot(selector.astype(wide).T, run_grad, precision=lax.Precision.HIGHEST) * scale_by
    )
    whole_grad = lax.psum(table_grad, ("dp", "ctx"))
    grad_filters = lax.psum_scatter(whole_grad, "tp", scatter_dimension=0, tiled=True)
    return (gated_out, grad_queries, grad_keys, grad_values, grad_filters)


def solution(mesh):
    in_specs = (
        P("dp", "tp", "ctx"),
        P("dp", "tp", "ctx"),
        P("dp", "tp", "ctx"),
        P("dp", "tp", "ctx"),
        P("tp", None),
        P("tp"),
    )
    out_specs = (
        P("dp", "tp", "ctx"),
        P("dp", "tp", "ctx"),
        P("dp", "tp", "ctx"),
        P("dp", "tp", "ctx"),
        P("tp", None),
    )
    return jax.shard_map(shards, mesh=mesh, in_specs=in_specs, out_specs=out_specs, check_vma=False)
```

profile of v0, /device:TPU:1, one launch (start us, length us, event | category | flops | bytes accessed | tf_op | source)
XLA Modules:
  0.0 434.3 jit_solution(4460730943248923558)
XLA Ops:
  14.5 5.6 %collective-permute-start = (bf16[2,2048,128]{2,1,0:T(8,128)(2,1)}, bf16[2,2048,128]{2,1,0:T(8,128)(2,1)}, u32[]{:S(2)}, u32[]{:S(2)}) collective-permute-start(bf16[2,2048,128]{2,1,0:T(8,128)(2,1)} %slice.89), channel_id=1, source_target_pairs={{0,4},{4,8},{8,12},{12,16},{16,20},{20,24},{24,28},{28,32},{32,36}... | collective-permute-start | bytes 3145736 | tf_op jit(solution)/shard_map/ppermute | solution.py:13
  30.5 10.8 %all_gather.3 = bf16[512,128]{1,0:T(8,128)(2,1)S(1)} all-gather(bf16[128,128]{1,0:T(8,128)(2,1)S(1)} %convert_element_type.105), channel_id=1, replica_groups=mesh['dp'=2,'ctx'=16,'tp'=4] {'tp'}, dimensions={0}, use_global_device_ids=true | all-gather | bytes 163840 | tf_op jit(solution)/shard_map/all_gather | solution.py:51
  42.0 4.5 %tile.4 = bf16[128,128,257]{0,2,1:T(8,128)(2,1)} broadcast(bf16[128,257]{0,1:T(8,128)(2,1)S(1)} %copy.57), dimensions={0,2} | broadcast | bytes 8487168 | tf_op jit(solution)/shard_map/tile | solution.py:65
  46.4 12.9 %tile.10 = bf16[128,32896]{0,1:T(8,128)(2,1)} reshape(bf16[128,128,257]{0,2,1:T(8,128)(2,1)} %tile.4) | data formatting | bytes 16842752 | tf_op jit(solution)/shard_map/tile | solution.py:65
  66.6 6.8 %copy.88 = bf16[128,128,128]{2,1,0:T(8,128)(2,1)} copy(bf16[128,128,128]{0,2,1:T(8,128)(2,1)} %get-tuple-element.6) | data formatting | bytes 8388608
  75.4 6.7 %copy.87 = bf16[128,128,128]{2,1,0:T(8,128)(2,1)} copy(bf16[128,128,128]{0,2,1:T(8,128)(2,1)} %get-tuple-element.5) | data formatting | bytes 8388608
  92.3 5.1 %reshape_squeeze.9 = bf16[128,16,3,128]{3,2,1,0:T(4,128)(2,1)} reshape(bf16[1,2048,384]{2,1,0:T(8,128)(2,1)} %get-tuple-element.22) | data formatting | bytes 3145728 | tf_op jit(solution)/shard_map/reshape;squeeze | solution.py:18
  97.4 5.2 %reshape_squeeze.8 = bf16[128,16,3,128]{3,2,1,0:T(4,128)(2,1)} reshape(bf16[1,2048,384]{2,1,0:T(8,128)(2,1)} %get-tuple-element.19) | data formatting | bytes 3145728 | tf_op jit(solution)/shard_map/reshape;squeeze | solution.py:18
  102.5 6.3 %convolution_bitcast_fusion = f32[128,128,128]{1,2,0:T(8,128)} fusion(bf16[128,16,3,128]{3,2,1,0:T(4,128)(2,1)} %reshape_squeeze.9, bf16[128,16,3,128]{3,2,1,0:T(4,128)(2,1)S(1)} %reshape_squeeze.21), kind=kOutput, calls=%fused_computation.19 | convolution fusion | flops 201326592 | bytes 11534336 | tf_op jit(solution)/shard_map/rmbi,rmbj->rij/dot_general | solution.py:37
  108.8 4.6 %convolution_bitcast_fusion.2 = f32[128,128,128]{1,2,0:T(8,128)} fusion(bf16[128,16,3,128]{3,2,1,0:T(4,128)(2,1)S(1)} %copy-done.9, bf16[128,16,3,128]{3,2,1,0:T(4,128)(2,1)S(1)} %copy-done.3), kind=kOutput, calls=%fused_computation.21 | convolution fusion | flops 201326592 | bytes 11534336 | tf_op jit(solution)/shard_map/rmbi,rmbj->rij/dot_general | solution.py:37
  117.7 5.1 %reshape.132 = bf16[128,16,3,128]{3,2,1,0:T(4,128)(2,1)} reshape(bf16[2048,384]{1,0:T(8,128)(2,1)} %get-tuple-element.28) | data formatting | bytes 3145728 | tf_op jit(solution)/shard_map/reshape | solution.py:18
  122.8 5.3 %reshape.131 = bf16[128,16,3,128]{3,2,1,0:T(4,128)(2,1)} reshape(bf16[2048,384]{1,0:T(8,128)(2,1)} %get-tuple-element.27) | data formatting | bytes 3145728 | tf_op jit(solution)/shard_map/reshape | solution.py:18
  128.1 6.3 %convolution_bitcast_fusion.1 = f32[128,128,128]{1,2,0:T(8,128)} fusion(bf16[128,16,3,128]{3,2,1,0:T(4,128)(2,1)} %reshape.132, bf16[128,16,3,128]{3,2,1,0:T(4,128)(2,1)S(1)} %reshape_squeeze.21), kind=kOutput, calls=%fused_computation.20 | convolution fusion | flops 201326592 | bytes 11534336 | tf_op jit(solution)/shard_map/rmbi,rmbj->rij/dot_general | solution.py:37
  134.4 4.7 %convolution_bitcast_fusion.3 = f32[128,128,128]{1,2,0:T(8,128)} fusion(bf16[128,16,3,128]{3,2,1,0:T(4,128)(2,1)S(1)} %copy-done.13, bf16[128,16,3,128]{3,2,1,0:T(4,128)(2,1)S(1)} %copy-done.4), kind=kOutput, calls=%fused_computation.22 | convolution fusion | flops 201326592 | bytes 11534336 | tf_op jit(solution)/shard_map/rmbi,rmbj->rij/dot_general | solution.py:37
  139.1 4.7 %fusion.4 = f32[128,16,3,128]{3,1,2,0:T(8,128)} fusion(bf16[128,128,128]{2,1,0:T(8,128)(2,1)S(1)} %copy-done.2, bf16[128,16,3,128]{3,2,1,0:T(4,128)(2,1)S(1)} %copy-done.12), kind=kOutput, calls=%fused_computation.7 | convolution fusion | flops 201326592 | bytes 8912896 | tf_op jit(solution)/shard_map/rmbj,rij->rmbi/dot_general | solution.py:21
  143.8 4.6 %fusion.6 = f32[128,16,3,128]{3,1,2,0:T(8,128)} fusion(bf16[128,128,128]{2,1,0:T(8,128)(2,1)S(1)} %copy-done.2, bf16[128,16,3,128]{3,2,1,0:T(4,128)(2,1)S(1)} %copy-done.13), kind=kOutput, calls=%fused_computation.9 | convolution fusion | flops 201326592 | bytes 8912896 | tf_op jit(solution)/shard_map/rmbj,rij->rmbi/dot_general | solution.py:21
  151.7 5.1 %reshape.133 = bf16[128,16,3,128]{3,2,1,0:T(4,128)(2,1)} reshape(bf16[2048,384]{1,0:T(8,128)(2,1)} %get-tuple-element.29) | data formatting | bytes 3145728 | tf_op jit(solution)/shard_map/reshape | solution.py:27
  166.6 6.0 %add.74 = f32[1,2048,384]{2,1,0:T(8,128)} reshape(f32[128,16,3,128]{3,2,1,0:T(4,128)} %copy.67) | data formatting | bytes 6291456 | tf_op jit(solution)/shard_map/add | solution.py:91
  172.7 5.3 %reshape.134 = bf16[128,16,3,128]{3,2,1,0:T(4,128)(2,1)} reshape(bf16[2048,384]{1,0:T(8,128)(2,1)} %get-tuple-element.30) | data formatting | bytes 3145728 | tf_op jit(solution)/shard_map/reshape | solution.py:27
  187.3 6.2 %add.76 = f32[1,2048,384]{2,1,0:T(8,128)} reshape(f32[128,16,3,128]{3,2,1,0:T(4,128)} %copy.70) | data formatting | bytes 6291456 | tf_op jit(solution)/shard_map/add | solution.py:91
  193.5 6.2 %fusion.19 = f32[128,16,3,128]{3,1,2,0:T(8,128)S(1)} fusion(f32[128,16,3,128]{3,1,2,0:T(8,128)} %fusion.4, bf16[128,128,128]{2,1,0:T(8,128)(2,1)} %copy.87, bf16[128,16,3,128]{3,2,1,0:T(4,128)(2,1)S(1)} %copy-done.11), kind=kOutput, calls=%fused_computation.37 | convolution fusion | flops 202113024 | bytes 12058624 | tf_op jit(solution)/shard_map/rmbj,rij->rmbi/dot_general | solution.py:21
  203.5 6.2 %add.72 = f32[1,2048,384]{2,1,0:T(8,128)} reshape(f32[128,16,3,128]{3,2,1,0:T(4,128)} %copy.64) | data formatting | bytes 6291456 | tf_op jit(solution)/shard_map/add | solution.py:87
  209.6 6.2 %fusion.16 = f32[128,16,3,128]{3,1,2,0:T(8,128)S(1)} fusion(f32[128,16,3,128]{3,1,2,0:T(8,128)} %fusion.6, bf16[128,128,128]{2,1,0:T(8,128)(2,1)} %copy.87, bf16[128,16,3,128]{3,2,1,0:T(4,128)(2,1)S(1)} %copy-done.10), kind=kOutput, calls=%fused_computation.36 | convolution fusion | flops 202113024 | bytes 12058624 | tf_op jit(solution)/shard_map/rmbj,rij->rmbi/dot_general | solution.py:21
  219.5 6.2 %add.70 = f32[1,2048,384]{2,1,0:T(8,128)} reshape(f32[128,16,3,128]{3,2,1,0:T(4,128)} %copy.61) | data formatting | bytes 6291456 | tf_op jit(solution)/shard_map/add | solution.py:87
  225.8 17.8 %maximum_add_fusion = f32[128,128,256]{1,2,0:T(8,128)} fusion(f32[128,128,128]{1,2,0:T(8,128)} %convolution_bitcast_fusion.2, f32[128,128,128]{1,2,0:T(8,128)} %convolution_bitcast_fusion.3, f32[128,128,128]{1,2,0:T(8,128)} %convolution_bitcast_fusion, f32[128,128,128]{1,2,0:T(8,128)} %convolution_bitcast_fusion.1), kind=kLoop, calls=%fused_computation | loop fusion | flops 12582912 | bytes 50331648 | tf_op jit(solution)/shard_map/add | solution.py:94
  243.6 17.6 %copy.79 = f32[128,128,256]{0,2,1:T(8,128)} copy(f32[128,128,256]{1,2,0:T(8,128)} %maximum_add_fusion) | data formatting | bytes 33554432 | tf_op jit(solution)/shard_map/add | solution.py:94
  261.2 13.3 %pad.4 = f32[128,32896]{0,1:T(8,128)} pad(f32[128,32768]{0,1:T(8,128)} %bitcast.67, f32[]{:T(128)} %constant.4.clone.1), padding=0_0x0_128 | pad | bytes 33619972 | tf_op jit(solution)/shard_map/jit(_pad)/pad | solution.py:106
  274.5 17.5 %reshape.135 = f32[128,128,257]{0,2,1:T(8,128)} reshape(f32[128,32896]{0,1:T(8,128)} %pad.4) | data formatting | bytes 33685504 | tf_op jit(solution)/shard_map/reshape | solution.py:107
  292.0 6.9 %reduce_sum.9 = f32[128,257]{0,1:T(8,128)S(1)} reduce(f32[128,128,257]{0,2,1:T(8,128)} %reshape.135, f32[]{:T(128)} %constant.4.clone.1), dimensions={1}, to_apply=%region_0.1 | reduce | flops 4177792 | bytes 16974340 | tf_op jit(solution)/shard_map/reduce_sum | solution.py:107
  300.1 4.5 %multiply_convert_fusion.3 = (bf16[1,2048,384]{2,1,0:T(8,128)(2,1)S(1)}, bf16[1,2048,384]{2,1,0:T(8,128)(2,1)S(1)}, bf16[1,2048,384]{2,1,0:T(8,128)(2,1)S(1)}, bf16[1,2048,384]{2,1,0:T(8,128)(2,1)S(1)}) fusion(f32[1,2048,384]{2,1,0:T(8,128)} %add.74, bf16[2,2048,384]{2,1,0:T(8,128)(2,1)} %param.7, f32[1,2048,384]{2,1,0:T(8,128)} %add.76, ...), kind=kLoop, calls=%fused_computation.28 | loop fusion | flops 9437184 | bytes 18874368 | tf_op jit(solution)/shard_map/convert_element_type | solution.py:93
  314.3 10.1 %reduce-scatter.2.cloned.1.call-done = f32[128,128]{1,0:T(8,128)} async-done(((f32[512,128]{1,0:T(8,128)}), f32[128,128]{1,0:T(8,128)}) %reduce-scatter.2.cloned.1.call-update) | async-done | bytes 65552 | tf_op jit(solution)/shard_map/reduce_scatter | solution.py:114
  326.5 99.2 %all-reduce.3.cloned.1.call-done = f32[128,128]{1,0:T(8,128)} async-done(((f32[128,128]{1,0:T(8,128)}), f32[128,128]{1,0:T(8,128)}) %all-reduce.3.cloned.1.call-update) | async-done | bytes 65552 | tf_op jit(solution)/shard_map/psum | solution.py:113
  (105 shorter events, 86.2 us)
Async XLA Ops:
  7.2 6.3 %copy-start.8 = (bf16[2,2048,384]{2,1,0:T(8,128)(2,1)S(1)}, bf16[2,2048,384]{2,1,0:T(8,128)(2,1)}, u32[]{:S(2)}) copy-start(bf16[2,2048,384]{2,1,0:T(8,128)(2,1)} %param.7) | copy-start | bytes 9437188
  7.2 317.3 %reduce-scatter.2.cloned.1.call-start = ((), (), s32[]{:S(2)}) async-start(), calls=%async_computation.1 | async-start | bytes 327680 | tf_op jit(solution)/shard_map/reduce_scatter | solution.py:114
  11.0 9.1 %copy-start.6 = (bf16[2,2048,384]{2,1,0:T(8,128)(2,1)S(1)}, bf16[2,2048,384]{2,1,0:T(8,128)(2,1)}, u32[]{:S(2)}) copy-start(bf16[2,2048,384]{2,1,0:T(8,128)(2,1)} %param.8) | copy-start | bytes 9437188
  12.0 136.4 %collective-permute-start.2 = (bf16[2,2048,128]{2,1,0:T(8,128)(2,1)}, bf16[2,2048,128]{2,1,0:T(8,128)(2,1)}, u32[]{:S(2)}, u32[]{:S(2)}) collective-permute-start(bf16[2,2048,128]{2,1,0:T(8,128)(2,1)} %slice.124), channel_id=1, source_target_pairs={{4,0},{8,4},{12,8},{16,12},{20,16},{24,20},{28,24},{32,28},{36,32}... | collective-permute-start | bytes 3145736 | tf_op jit(solution)/shard_map/ppermute | solution.py:13
  14.5 98.9 %collective-permute-start = (bf16[2,2048,128]{2,1,0:T(8,128)(2,1)}, bf16[2,2048,128]{2,1,0:T(8,128)(2,1)}, u32[]{:S(2)}, u32[]{:S(2)}) collective-permute-start(bf16[2,2048,128]{2,1,0:T(8,128)(2,1)} %slice.89), channel_id=1, source_target_pairs={{0,4},{4,8},{8,12},{12,16},{16,20},{20,24},{24,28},{28,32},{32,36}... | collective-permute-start | bytes 3145736 | tf_op jit(solution)/shard_map/ppermute | solution.py:13
  21.1 92.3 %collective-permute-start.1 = (bf16[2,2048,128]{2,1,0:T(8,128)(2,1)}, bf16[2,2048,128]{2,1,0:T(8,128)(2,1)}, u32[]{:S(2)}, u32[]{:S(2)}) collective-permute-start(bf16[2,2048,128]{2,1,0:T(8,128)(2,1)} %slice.90), channel_id=1, source_target_pairs={{0,4},{4,8},{8,12},{12,16},{16,20},{20,24},{24,28},{28,32},{32,36}... | collective-permute-start | bytes 3145736 | tf_op jit(solution)/shard_map/ppermute | solution.py:13
  29.1 1.1 copy-start.23
  29.1 1.3 copy-start.22
  59.4 3.4 slice-start
  66.6 6.8 %copy-start.18 = (bf16[1,2048,384]{2,1,0:T(8,128)(2,1)S(1)}, bf16[1,2048,384]{2,1,0:T(8,128)(2,1)}, u32[]{:S(2)}) copy-start(bf16[1,2048,384]{2,1,0:T(8,128)(2,1)} %get-tuple-element.11) | copy-start | bytes 4718596
  102.5 6.3 %copy-start.3 = (bf16[128,16,3,128]{3,2,1,0:T(4,128)(2,1)S(1)}, bf16[128,16,3,128]{3,2,1,0:T(4,128)(2,1)}, u32[]{:S(2)}) copy-start(bf16[128,16,3,128]{3,2,1,0:T(4,128)(2,1)} %reshape_squeeze.20) | copy-start | bytes 4718596
  102.5 6.3 %copy-start.9 = (bf16[128,16,3,128]{3,2,1,0:T(4,128)(2,1)S(1)}, bf16[128,16,3,128]{3,2,1,0:T(4,128)(2,1)}, u32[]{:S(2)}) copy-start(bf16[128,16,3,128]{3,2,1,0:T(4,128)(2,1)} %reshape_squeeze.8) | copy-start | bytes 4718596
  113.4 2.1 copy-start.20
  113.4 2.2 copy-start.21
  128.1 6.3 %copy-start.4 = (bf16[128,16,3,128]{3,2,1,0:T(4,128)(2,1)S(1)}, bf16[128,16,3,128]{3,2,1,0:T(4,128)(2,1)}, u32[]{:S(2)}) copy-start(bf16[128,16,3,128]{3,2,1,0:T(4,128)(2,1)} %reshape_squeeze.20) | copy-start | bytes 4718596
  128.1 6.3 %copy-start.13 = (bf16[128,16,3,128]{3,2,1,0:T(4,128)(2,1)S(1)}, bf16[128,16,3,128]{3,2,1,0:T(4,128)(2,1)}, u32[]{:S(2)}) copy-start(bf16[128,16,3,128]{3,2,1,0:T(4,128)(2,1)} %reshape.131) | copy-start | bytes 4718596
  134.4 4.8 %copy-start.2 = (bf16[128,128,128]{2,1,0:T(8,128)(2,1)S(1)}, bf16[128,128,128]{2,1,0:T(8,128)(2,1)}, u32[]{:S(2)}) copy-start(bf16[128,128,128]{2,1,0:T(8,128)(2,1)} %copy.88) | copy-start | bytes 12582916
  134.4 4.8 %copy-start.12 = (bf16[128,16,3,128]{3,2,1,0:T(4,128)(2,1)S(1)}, bf16[128,16,3,128]{3,2,1,0:T(4,128)(2,1)}, u32[]{:S(2)}) copy-start(bf16[128,16,3,128]{3,2,1,0:T(4,128)(2,1)} %reshape.132) | copy-start | bytes 4718596
  143.8 5.9 %copy-start.19 = (bf16[2048,256]{1,0:T(8,128)(2,1)S(1)}, bf16[2048,256]{1,0:T(8,128)(2,1)}, u32[]{:S(2)}) copy-start(bf16[2048,256]{1,0:T(8,128)(2,1)} %slice.127) | copy-start | bytes 3145732
  156.8 4.2 copy-start
  156.8 4.7 %copy-start.5 = (bf16[128,16,3,128]{3,2,1,0:T(4,128)(2,1)S(1)}, bf16[128,16,3,128]{3,2,1,0:T(4,128)(2,1)}, u32[]{:S(2)}) copy-start(bf16[128,16,3,128]{3,2,1,0:T(4,128)(2,1)} %reshape_squeeze.20) | copy-start | bytes 4718596
  178.0 4.2 copy-start.1
  187.3 6.2 %copy-start.11 = (bf16[128,16,3,128]{3,2,1,0:T(4,128)(2,1)S(1)}, bf16[128,16,3,128]{3,2,1,0:T(4,128)(2,1)}, u32[]{:S(2)}) copy-start(bf16[128,16,3,128]{3,2,1,0:T(4,128)(2,1)} %reshape_squeeze.9) | copy-start | bytes 4718596
  203.5 6.2 %copy-start.10 = (bf16[128,16,3,128]{3,2,1,0:T(4,128)(2,1)S(1)}, bf16[128,16,3,128]{3,2,1,0:T(4,128)(2,1)}, u32[]{:S(2)}) copy-start(bf16[128,16,3,128]{3,2,1,0:T(4,128)(2,1)} %reshape_squeeze.8) | copy-start | bytes 4718596
  292.0 8.1 %copy-start.7 = (bf16[2,2048,384]{2,1,0:T(8,128)(2,1)S(1)}, bf16[2,2048,384]{2,1,0:T(8,128)(2,1)}, u32[]{:S(2)}) copy-start(bf16[2,2048,384]{2,1,0:T(8,128)(2,1)} %param.8) | copy-start | bytes 9437188
  300.0 125.7 %all-reduce.3.cloned.1.call-start = ((), (), s32[]{:S(2)}) async-start(), calls=%async_computation.2 | async-start | bytes 131072 | tf_op jit(solution)/shard_map/psum | solution.py:113
  300.1 6.6 %copy-start.16 = (bf16[2,2048,384]{2,1,0:T(8,128)(2,1)S(1)}, bf16[2,2048,384]{2,1,0:T(8,128)(2,1)}, u32[]{:S(2)}) copy-start(bf16[2,2048,384]{2,1,0:T(8,128)(2,1)} %param.9) | copy-start | bytes 9437188
  300.1 6.6 %copy-start.17 = (bf16[2,2048,384]{2,1,0:T(8,128)(2,1)S(1)}, bf16[2,2048,384]{2,1,0:T(8,128)(2,1)}, u32[]{:S(2)}) copy-start(bf16[2,2048,384]{2,1,0:T(8,128)(2,1)} %param.6) | copy-start | bytes 9437188
  304.6 3.4 copy-start.14
  304.6 4.2 copy-start.15
Sparse Core Ops, SparseCore 0:
  300.1 24.3 reduce-scatter.1
  328.1 97.5 all-reduce.2
where the time goes:
time: 440 us; the launch traced here: 434 us
  local copies, waits for them, and re-layouts  182 us (41%)
  waiting for transfers between devices  109 us (25%)
  matrix products  55.8 us (13%)
  other arithmetic  51 us (12%)
  between operations  14.6 us (3%)
  blocking collectives  10.8 us (2%)
  starting transfers between devices  10.4 us (2%)
    psum x1, waiting for transfers between devices, shards(): whole_grad = lax.psum(table_grad, ('dp', 'ctx'))  99.2 us
    dot_general x4, matrix products, band_outer(): jnp.einsum('rmbi,rmbj->rij', left_rows.reshape(shape_four), right_rows.re...  21.9 us
    dot_general x4, matrix products, band_apply(): jnp.einsum('rmbj,rij->rmbi', blocked, matrix, preferred_element_type=jnp....  21.6 us
    add x4, local copies, waits for them, and re-layouts, shards(): mixed_rows + band_apply(lower_band, previous, block_rows, groups_here)  19.9 us
    add x4, local copies, waits for them, and re-layouts, shards(): upward + band_adjoint(lower_band, following, block_rows, groups_here)  19.8 us
    unnamed x51, local copies, waits for them, and re-layouts  17.9 us
    add x1, other arithmetic, shards(): outer_total + jnp.concatenate([band_outer(backward_w, previous, block_row...  17.8 us
    add x1, local copies, waits for them, and re-layouts, shards(): outer_total + jnp.concatenate([band_outer(backward_w, previous, block_row...  17.6 us
  transfers between devices with their start and end apart: 5, of which 2 were waited for; matrix products, arithmetic and copies ran while one was open for 29% of the time, Pallas kernels for 0%

commit v1 on v0

v1 whole, which is shorter than its diff:
```python
import jax
import jax.numpy as jnp
from jax import lax
from jax.experimental import pallas as pl
from jax.experimental.pallas import tpu as pltpu
from jax.sharding import PartitionSpec as P

BF16 = jnp.bfloat16
F32 = jnp.float32
TAPS = 128
MEMBERS = 16
GROUPS = 512
CHUNKS = 16
AHEAD = 3
FIRST = 8
MESH = pl.DeviceIdType.MESH


def aligned(index, size):
    return pl.ds(pl.multiple_of(index * size, size), size)


def shards(queries, key_proj, value_proj, grad_output, filters, group_of, tokens, nx):
    windows, channels, positions = queries.shape
    runs = channels // MEMBERS
    blocks = positions // TAPS
    width = channels // CHUNKS
    chunk_runs = width // MEMBERS
    stack = windows * MEMBERS
    half = runs // 2
    ctx_size = lax.axis_size("ctx")
    tp_size = lax.axis_size("tp")
    ny = ctx_size // nx
    scale_by = 1.0 / tokens

    def body(
        filt_ref, grp_ref, q_hbm, k_hbm, v_hbm, g_hbm,
        gated, gradq, gradk, gradv, gradf,
        q, k, v, g, u_out, d_out, u_in, d_in, circs, masks, table, groups, taps_of,
        partial, local, core_in, y_all, x_all, whole, z_all,
        edge_sem, rest_sem, halo_send, halo_recv, table_send, table_recv,
        core_send, core_recv, y_send, y_recv, x_send, x_recv, z_send, z_recv,
    ):
        dp = lax.axis_index("dp")
        ctx = lax.axis_index("ctx")
        tp = lax.axis_index("tp")
        y = ctx // nx
        x = lax.rem(ctx, nx)
        after = {"ctx": lax.rem(ctx + 1, ctx_size)}
        before = {"ctx": lax.rem(ctx + ctx_size - 1, ctx_size)}
        other = {"dp": 1 - dp}
        y_peers = [{"ctx": lax.rem(y + i, ny) * nx + x} for i in range(1, ny)]
        x_peers = [{"ctx": y * nx + lax.rem(x + i, nx)} for i in range(1, nx)]
        z_peers = [{"tp": lax.rem(tp + i, tp_size)} for i in range(1, tp_size)]
        peers = [after, before] + z_peers + x_peers + y_peers + [other]
        barrier = pltpu.get_barrier_semaphore()
        for peer in peers:
            pl.semaphore_signal(barrier, 1, device_id=peer, device_id_type=MESH)

        hbm = [k_hbm, v_hbm, q_hbm, g_hbm]
        vmem = [k, v, q, g]
        edge_lane = [positions - TAPS, positions - TAPS, 0, 0]
        rest_lane = [0, 0, TAPS, TAPS]
        pieces = 4
        piece = channels // pieces

        def edge_copy(a, p):
            part = (slice(None), pl.ds(p * piece, piece), pl.ds(edge_lane[a], TAPS))
            return pltpu.make_async_copy(hbm[a].at[part], vmem[a].at[part], edge_sem.at[a, p])

        def rest_copy(a, c):
            part = (slice(None), aligned(c, width), pl.ds(rest_lane[a], positions - TAPS))
            return pltpu.make_async_copy(hbm[a].at[part], vmem[a].at[part], rest_sem.at[a, c])

        for p in range(pieces):
            for a, at in ((0, p), (1, p), (2, pieces - 1 - p), (3, pieces - 1 - p)):
                edge_copy(a, at).start()

        def start_rest(i, carry):
            for a in range(4):
                rest_copy(a, i).start()
                rest_copy(a, CHUNKS - 1 - i).start()
            return carry

        lax.fori_loop(0, CHUNKS // 2, start_rest, 0)

        row = lax.broadcasted_iota(jnp.int32, (TAPS, TAPS), 0)
        lane = lax.broadcasted_iota(jnp.int32, (TAPS, TAPS), 1)
        masks[0] = jnp.where(lane >= row, 1.0, 0.0).astype(BF16)
        masks[1] = jnp.where(lane < row, 1.0, 0.0).astype(BF16)
        table[tp] = filt_ref[...].astype(BF16)
        groups[tp] = grp_ref[...]
        has_after = jnp.where(ctx < ctx_size - 1, 1.0, 0.0).astype(F32)
        has_before = jnp.where(ctx > 0, 1.0, 0.0).astype(F32)

        for p in range(pieces):
            at = pieces - 1 - p
            edge_copy(0, p).wait()
            edge_copy(1, p).wait()
            ch = pl.ds(p * piece, piece)
            ln = pl.ds(positions - TAPS, TAPS)
            scaled = k[:, ch, ln].astype(F32) * v[:, ch, ln].astype(F32) * has_after
            u_out[:, ch, :] = scaled.astype(BF16)
            edge_copy(2, at).wait()
            edge_copy(3, at).wait()
            ch = pl.ds(at * piece, piece)
            ln = pl.ds(0, TAPS)
            scaled = q[:, ch, ln].astype(F32) * g[:, ch, ln].astype(F32) * has_before
            d_out[:, ch, :] = scaled.astype(BF16)

        pl.semaphore_wait(barrier, len(peers))

        def u_copy(c):
            part = (slice(None), aligned(c, width), slice(None))
            return pltpu.make_async_remote_copy(
                u_out.at[part], u_in.at[part], halo_send.at[0, c], halo_recv.at[0, c],
                device_id=after, device_id_type=MESH,
            )

        def d_copy(c):
            part = (slice(None), aligned(c, width), slice(None))
            return pltpu.make_async_remote_copy(
                d_out.at[part], d_in.at[part], halo_send.at[1, c], halo_recv.at[1, c],
                device_id=before, device_id_type=MESH,
            )

        def start_halo(i):
            u_copy(i).start()
            d_copy(CHUNKS - 1 - i).start()

        start_halo(0)

        def table_copies(i):
            return [
                pltpu.make_async_remote_copy(
                    ref.at[tp], ref.at[tp], table_send.at[j, i], table_recv.at[j, i],
                    device_id=z_peers[i], device_id_type=MESH,
                )
                for j, ref in enumerate((table, groups))
            ]

        for i in range(tp_size - 1):
            for copy in table_copies(i):
                copy.start()

        def start_more(i, carry):
            start_halo(i)
            return carry

        lax.fori_loop(1, FIRST, start_more, 0)

        def advance(step):
            @pl.when(jnp.logical_and(step + AHEAD >= FIRST, step + AHEAD < CHUNKS))
            def _():
                start_halo(step + AHEAD)

        for i in range(tp_size - 1):
            for copy in table_copies(i):
                copy.wait()

        def run_groups(z):
            ids = groups[z]
            span = TAPS // MEMBERS
            pick = jnp.where(
                lax.broadcasted_iota(jnp.int32, (runs, channels // TAPS), 1)
                == lax.broadcasted_iota(jnp.int32, (runs, channels // TAPS), 0) // span,
                1.0, 0.0,
            ).astype(BF16)
            high = jnp.dot(pick, (ids >> 4).astype(F32).astype(BF16), preferred_element_type=F32)
            low = jnp.dot(pick, (ids & 15).astype(F32).astype(BF16), preferred_element_type=F32)
            r = lax.broadcasted_iota(jnp.int32, (runs, TAPS), 0)
            l = lax.broadcasted_iota(jnp.int32, (runs, TAPS), 1)
            keep = jnp.where(l == (r % span) * MEMBERS, high * 16.0 + low, 0.0)
            return jnp.sum(keep, axis=1, keepdims=True)

        mine = run_groups(tp)
        rows_here = GROUPS // tp_size
        chosen = jnp.zeros((runs, TAPS), F32)
        for z in range(tp_size):
            ids = lax.broadcasted_iota(jnp.int32, (runs, rows_here), 1) + z * rows_here
            onehot = jnp.where(ids.astype(F32) == mine, 1.0, 0.0).astype(BF16)
            chosen = chosen + jnp.dot(onehot, table[z], preferred_element_type=F32)
        taps_of[...] = chosen

        nothing = jnp.zeros((stack, TAPS), BF16)

        def run_rows(ref, r, b):
            return jnp.concatenate(
                [ref[w, aligned(r, MEMBERS), TAPS * b : TAPS * b + TAPS] for w in range(windows)], axis=0
            )

        def product(left, right, r):
            return [run_rows(left, r, b) * run_rows(right, r, b) for b in range(blocks)]

        def put(out, gate, r, value):
            for b in range(blocks):
                for w in range(windows):
                    at = (w, aligned(r, MEMBERS), slice(TAPS * b, TAPS * b + TAPS))
                    first = b * stack + w * MEMBERS
                    out[at] = (gate[at].astype(F32) * value[first : first + MEMBERS]).astype(BF16)

        def circulant(r):
            rows = jnp.broadcast_to(taps_of[pl.ds(r, 1), :], (TAPS, TAPS))
            made = pltpu.roll(rows, 0, 1, stride=1, stride_axis=0).astype(BF16)
            circs[r] = made
            return made

        def outer(u_four, d_four, r):
            left = jnp.concatenate(u_four, axis=0)
            shifted = [nothing] + d_four
            right = jnp.concatenate(
                [jnp.concatenate([shifted[i + 1], shifted[i]], axis=1) for i in range(blocks + 1)], axis=0
            )
            pairs = lax.dot_general(left, right, (((0,), (0,)), ((), ())), preferred_element_type=F32)
            folded = jnp.where(lane >= row, pairs[:, TAPS:], pairs[:, :TAPS])
            total = folded[0:8]
            for i in range(1, TAPS // 8):
                total = total + pltpu.roll(folded[8 * i : 8 * i + 8], TAPS - 8 * i, 1)
            partial[aligned(r, 8), :] = total

        def forward(u_four, circ, r):
            weights = jnp.concatenate([circ * masks[1], circ * masks[0]], axis=0)
            left = jnp.concatenate(
                [jnp.concatenate([u_four[b], u_four[b + 1]], axis=1) for b in range(blocks)], axis=0
            )
            mixed = jnp.dot(left, weights, preferred_element_type=F32)
            put(gated, q, r, mixed)
            put(gradq, g, r, mixed)

        def backward(d_four, circ, r):
            weights = jnp.concatenate([circ * masks[0], circ * masks[1]], axis=1)
            left = jnp.concatenate(
                [jnp.concatenate([d_four[b], d_four[b + 1]], axis=1) for b in range(blocks)], axis=0
            )
            upward = lax.dot_general(left, weights, (((1,), (1,)), ((), ())), preferred_element_type=F32)
            put(gradk, v, r, upward)
            put(gradv, k, r, upward)

        def front_first(r):
            circ = circulant(r)
            u_four = [run_rows(u_in, r, 0)] + product(k, v, r)
            outer(u_four, product(g, q, r) + [nothing], r)
            forward(u_four, circ, r)

        def back_first(r):
            circ = circulant(r)
            d_four = product(g, q, r) + [run_rows(d_in, r, 0)]
            outer([nothing] + product(k, v, r), d_four, r)
            backward(d_four, circ, r)

        unroll = 4

        def first_phase(step, carry):
            back = CHUNKS - 1 - step
            for a in range(4):
                rest_copy(a, step).wait()
                rest_copy(a, back).wait()
            u_copy(step).wait_recv()
            d_copy(back).wait_recv()
            advance(step)

            def some(i, inner):
                for j in range(unroll):
                    front_first(step * chunk_runs + i * unroll + j)
                    back_first(back * chunk_runs + i * unroll + j)
                return inner

            return lax.fori_loop(0, chunk_runs // unroll, some, carry)

        lax.fori_loop(0, CHUNKS // 2, first_phase, 0)

        def second_phase(step, carry):
            back = CHUNKS - 1 - step
            u_copy(step).wait_recv()
            d_copy(back).wait_recv()
            advance(step)

            def some(i, inner):
                for j in range(unroll):
                    r = step * chunk_runs + i * unroll + j
                    forward([run_rows(u_in, r, 0)] + product(k, v, r), circs[r], r)
                    r = back * chunk_runs + i * unroll + j
                    backward(product(g, q, r) + [run_rows(d_in, r, 0)], circs[r], r)
                return inner

            return lax.fori_loop(0, chunk_runs // unroll, some, carry)

        total = partial[pl.ds(0, runs, stride=8), :]
        for s in range(1, 8):
            total = total + pltpu.roll(partial[pl.ds(s, runs, stride=8), :], TAPS - s, 1)
        local[...] = total
        own = aligned(dp, half)
        theirs = aligned(1 - dp, half)
        core_copy = pltpu.make_async_remote_copy(
            local.at[theirs], core_in, core_send.at[0], core_recv.at[0], device_id=other, device_id_type=MESH
        )
        core_copy.start()
        middle = CHUNKS // 2
        lax.fori_loop(middle, middle + 1, second_phase, 0)

        def spread(ref, slot, send, recv, to):
            return [
                pltpu.make_async_remote_copy(
                    ref.at[slot], ref.at[slot], send.at[i], recv.at[i], device_id=peer, device_id_type=MESH
                )
                for i, peer in enumerate(to)
            ]

        core_copy.wait()
        y_all[y] = local[own, :] + core_in[...]
        y_copies = spread(y_all, y, y_send, y_recv, y_peers)
        for copy in y_copies:
            copy.start()
        lax.fori_loop(middle + 1, middle + 3, second_phase, 0)
        for copy in y_copies:
            copy.wait()
        summed = y_all[0]
        for i in range(1, ny):
            summed = summed + y_all[i]
        x_all[x] = summed
        x_copies = spread(x_all, x, x_send, x_recv, x_peers)
        for copy in x_copies:
            copy.start()
        lax.fori_loop(middle + 3, middle + 6, second_phase, 0)
        for copy in x_copies:
            copy.wait()
        summed = x_all[0]
        for i in range(1, nx):
            summed = summed + x_all[i]
        z_all[tp, own, :] = summed
        core_back = pltpu.make_async_remote_copy(
            z_all.at[tp, own, :], z_all.at[tp, own, :], core_send.at[1], core_recv.at[1],
            device_id=other, device_id_type=MESH,
        )
        core_back.start()
        lax.fori_loop(middle + 6, middle + 7, second_phase, 0)
        core_back.wait()
        z_copies = spread(z_all, tp, z_send, z_recv, z_peers)
        for copy in z_copies:
            copy.start()
        lax.fori_loop(middle + 7, middle + 8, second_phase, 0)
        for copy in z_copies:
            copy.wait()
        result = jnp.zeros((rows_here, TAPS), F32)
        first_row = tp * rows_here
        for z in range(tp_size):
            ids = lax.broadcasted_iota(jnp.int32, (runs, rows_here), 1) + first_row
            onehot = jnp.where(ids.astype(F32) == run_groups(z), 1.0, 0.0).astype(BF16)
            rest = z_all[z]
            for _ in range(3):
                piece_of = rest.astype(BF16)
                rest = rest - piece_of.astype(F32)
                result = result + lax.dot_general(
                    onehot, piece_of, (((0,), (0,)), ((), ())), preferred_element_type=F32
                )
        gradf[...] = result * scale_by

        def finish(i, carry):
            u_copy(i).wait_send()
            d_copy(i).wait_send()
            return carry

        lax.fori_loop(0, CHUNKS, finish, 0)

    resident = pl.BlockSpec(memory_space=pltpu.VMEM)
    remote = pl.BlockSpec(memory_space=pltpu.HBM)
    big = (windows, channels, positions)
    halo = (windows, channels, TAPS)
    dma = pltpu.SemaphoreType.DMA
    results = pl.pallas_call(
        body,
        out_shape=[pltpu.VMEM(big, BF16)] * 4 + [jax.ShapeDtypeStruct((GROUPS // tp_size, TAPS), F32)],
        in_specs=[resident, resident] + [remote] * 4,
        out_specs=[resident] * 5,
        scratch_shapes=[pltpu.VMEM(big, BF16)] * 4
        + [pltpu.VMEM(halo, BF16)] * 4
        + [
            pltpu.VMEM((runs, TAPS, TAPS), BF16),
            pltpu.VMEM((2, TAPS, TAPS), BF16),
            pltpu.VMEM((tp_size, GROUPS // tp_size, TAPS), BF16),
            pltpu.VMEM((tp_size, channels // TAPS, TAPS), jnp.int32),
            pltpu.VMEM((runs, TAPS), F32),
            pltpu.VMEM((runs * 8, TAPS), F32),
            pltpu.VMEM((runs, TAPS), F32),
            pltpu.VMEM((half, TAPS), F32),
            pltpu.VMEM((ny, half, TAPS), F32),
            pltpu.VMEM((nx, half, TAPS), F32),
            pltpu.VMEM((8, TAPS), F32),
            pltpu.VMEM((tp_size, runs, TAPS), F32),
            dma((4, 4)), dma((4, CHUNKS)), dma((2, CHUNKS)), dma((2, CHUNKS)), dma((2, tp_size - 1)), dma((2, tp_size - 1)),
            dma((2,)), dma((2,)), dma((ny - 1,)), dma((ny - 1,)), dma((nx - 1,)), dma((nx - 1,)),
            dma((tp_size - 1,)), dma((tp_size - 1,)),
        ],
        compiler_params=pltpu.CompilerParams(collective_id=0, has_side_effects=True, vmem_limit_bytes=42 << 20),
    )(filters, group_of.reshape(channels // TAPS, TAPS), queries, key_proj, value_proj, grad_output)

    def write(*refs):
        ins, outs, sem = refs[:4], refs[4:8], refs[8]
        copies = [
            pltpu.make_async_copy(ins[a].at[w], outs[a].at[w], sem.at[a, w])
            for a in range(4)
            for w in range(windows)
        ]
        for copy in copies:
            copy.start()
        for copy in copies:
            copy.wait()

    held = [pltpu.with_memory_space_constraint(r, pltpu.VMEM) for r in results[:4]]
    written = pl.pallas_call(
        write,
        out_shape=[jax.ShapeDtypeStruct(big, BF16)] * 4,
        in_specs=[resident] * 4,
        out_specs=[remote] * 4,
        scratch_shapes=[dma((4, windows))],
        compiler_params=pltpu.CompilerParams(vmem_limit_bytes=4 << 20),
    )(*held)
    return (*written, results[4])


def solution(mesh):
    spec = P("dp", "tp", "ctx")
    nx = 4

    def call(queries, key_proj, value_proj, grad_output, filters, group_of):
        tokens = queries.shape[0] * queries.shape[2]

        def local(*args):
            return shards(*args, tokens, nx)

        return jax.shard_map(
            local,
            mesh=mesh,
            in_specs=(spec, spec, spec, spec, P("tp", None), P("tp")),
            out_specs=(spec, spec, spec, spec, P("tp", None)),
            check_vma=False,
        )(queries, key_proj, value_proj, grad_output, filters, group_of)

    return call
```

time: 440 us -> 52.8 us (0.12)
  the two profiles are of different devices: /device:TPU:1 before, /device:TPU:0 now
where the time goes in v1:
time: 52.8 us; the launch traced here: 52.6 us
  Pallas kernels  51.3 us (97%)
  between operations  0.66 us (1%)
  local copies, waits for them, and re-layouts  0.64 us (1%)
    pallas_call x1, Pallas kernels, shards(): pl.pallas_call(body, out_shape=[pltpu.VMEM(big, BF16)] * 4 + [jax.ShapeDt...  46.7 us
    pallas_call x1, Pallas kernels, shards(): pl.pallas_call(write, out_shape=[jax.ShapeDtypeStruct(big, BF16)] * 4, in...  4.66 us

profile of v1, /device:TPU:0, one launch (start us, length us, event | category | flops | bytes accessed | tf_op | source)
XLA Modules:
  0.0 52.6 jit_solution(10823437287663686912)
XLA Ops:
  0.6 46.7 %shard_map.101 = (bf16[2,2048,384]{2,1,0:T(8,128)(2,1)S(1)}, bf16[2,2048,384]{2,1,0:T(8,128)(2,1)S(1)}, bf16[2,2048,384]{2,1,0:T(8,128)(2,1)S(1)}, bf16[2,2048,384]{2,1,0:T(8,128)(2,1)S(1)}, f32[128,128]{1,0:T(8,128)}) custom-call(f32[128,128]{1,0:T(8,128)} %filt_ref.1, s32[16,128]{1,0:T(8,128)} %bitcast.1, bf16[2,2048,384]{2,1,0:T(8,128)(2,1)} %q_hbm.1, ...), custom_call_target="tpu_custom_call" | custom-call | tf_op jit(solution)/shard_map/pallas_call | solution.py:370
  47.3 0.0 copy-start
  47.3 4.7 %shard_map.102 = (bf16[2,2048,384]{2,1,0:T(8,128)(2,1)}, bf16[2,2048,384]{2,1,0:T(8,128)(2,1)}, bf16[2,2048,384]{2,1,0:T(8,128)(2,1)}, bf16[2,2048,384]{2,1,0:T(8,128)(2,1)}) custom-call(bf16[2,2048,384]{2,1,0:T(8,128)(2,1)S(1)} %get-tuple-element.14.refs_0_, bf16[2,2048,384]{2,1,0:T(8,128)(2,1)S(1)} %get-tuple-element.15.refs_1_, ...), custom_call_target="tpu_custom_call" | custom-call | tf_op jit(solution)/shard_map/pallas_call | solution.py:410
  52.0 0.0 copy-done
  52.0 0.6 %copy.12 = f32[128,128]{1,0:T(8,128)} copy(f32[128,128]{1,0:T(8,128)S(1)} %copy-done) | data formatting | bytes 131072
Async XLA Ops:
  47.3 4.7 %copy-start = (f32[128,128]{1,0:T(8,128)S(1)}, f32[128,128]{1,0:T(8,128)}, u32[]{:S(2)}) copy-start(f32[128,128]{1,0:T(8,128)} %get-tuple-element.32) | copy-start | bytes 196612

commit v2 on v1

v2 whole, which is shorter than its diff:
```python
import jax
import jax.numpy as jnp
from jax import lax
from jax.experimental import pallas as pl
from jax.experimental.pallas import tpu as pltpu
from jax.sharding import PartitionSpec as P

BF16 = jnp.bfloat16
F32 = jnp.float32
TAPS = 128
MEMBERS = 16
GROUPS = 512
CHUNKS = 16
EARLY = 2
LATER = 5
EDGES = (0, 1, 4, 8, 16)
PARTS = 1
STEPS = (1, 8)
MESH = pl.DeviceIdType.MESH


def aligned(index, size):
    return pl.ds(pl.multiple_of(index * size, size), size)


def shards(queries, key_proj, value_proj, grad_output, filters, group_of, tokens, nx):
    windows, channels, positions = queries.shape
    runs = channels // MEMBERS
    blocks = positions // TAPS
    width = channels // CHUNKS
    chunk_runs = width // MEMBERS
    stack = windows * MEMBERS
    half = runs // 2
    ctx_size = lax.axis_size("ctx")
    tp_size = lax.axis_size("tp")
    ny = ctx_size // nx
    scale_by = 1.0 / tokens

    def body(
        filt_ref, grp_ref, q_hbm, k_hbm, v_hbm, g_hbm,
        gated, gradq, gradk, gradv, gradf,
        q, k, v, g, u_out, d_out, u_in, d_in, masks, table, groups, taps_of, routes,
        partial, local, core_in, y_all, x_all, z_all, routed, both,
        edge_sem, rest_sem, halo_send, halo_recv, table_send, table_recv,
        known, core_send, core_recv, y_send, y_recv, x_send, x_recv, z_send, z_recv, last_send, last_recv,
    ):
        dp = lax.axis_index("dp")
        ctx = lax.axis_index("ctx")
        tp = lax.axis_index("tp")
        y = ctx // nx
        x = lax.rem(ctx, nx)
        after = {"ctx": lax.rem(ctx + 1, ctx_size)}
        before = {"ctx": lax.rem(ctx + ctx_size - 1, ctx_size)}
        other = {"dp": 1 - dp}
        y_peers = [{"ctx": lax.rem(y + i, ny) * nx + x} for i in range(1, ny)]
        x_peers = [{"ctx": y * nx + lax.rem(x + i, nx)} for i in range(1, nx)]
        z_peers = [{"tp": lax.rem(tp + i, tp_size)} for i in range(1, tp_size)]
        last_peers = [other] + z_peers + [{"dp": 1 - dp, **peer} for peer in z_peers]
        greeted = [after, before, other] + z_peers
        barrier = pltpu.get_barrier_semaphore()
        for peer in greeted:
            pl.semaphore_signal(barrier, 1, device_id=peer, device_id_type=MESH)

        def along(distance):
            return {"ctx": lax.rem(ctx + distance + ctx_size, ctx_size)}

        def pass_on(round_of, to):
            for peer in to:
                pl.semaphore_signal(known.at[round_of], 1, device_id=peer, device_id_type=MESH)

        hbm = [k_hbm, v_hbm, q_hbm, g_hbm]
        vmem = [k, v, q, g]
        edge_lane = [positions - TAPS, positions - TAPS, 0, 0]
        rest_lane = [0, 0, TAPS, TAPS]
        pieces = len(EDGES) - 1

        def edge_rows(a, p):
            low, high = EDGES[p] * width, EDGES[p + 1] * width
            return pl.ds(low, high - low) if a < 2 else pl.ds(channels - high, high - low)

        def edge_copy(a, p):
            part = (slice(None), edge_rows(a, p), pl.ds(edge_lane[a], TAPS))
            return pltpu.make_async_copy(hbm[a].at[part], vmem[a].at[part], edge_sem.at[a, p])

        def rest_copy(a, c):
            part = (slice(None), aligned(c, width), pl.ds(rest_lane[a], positions - TAPS))
            return pltpu.make_async_copy(hbm[a].at[part], vmem[a].at[part], rest_sem.at[a, c])

        for p in range(pieces):
            for a in range(4):
                edge_copy(a, p).start()

        def start_rest(i, carry):
            for a in range(4):
                rest_copy(a, i).start()
                rest_copy(a, CHUNKS - 1 - i).start()
            return carry

        def u_copy(c):
            part = (slice(None), aligned(c, width), slice(None))
            return pltpu.make_async_remote_copy(
                u_out.at[part], u_in.at[part], halo_send.at[0, c], halo_recv.at[0, c],
                device_id=after, device_id_type=MESH,
            )

        def d_copy(c):
            part = (slice(None), aligned(c, width), slice(None))
            return pltpu.make_async_remote_copy(
                d_out.at[part], d_in.at[part], halo_send.at[1, c], halo_recv.at[1, c],
                device_id=before, device_id_type=MESH,
            )

        not_first = ctx > 0
        not_last = ctx < ctx_size - 1

        def start_halo(i, carry):
            @pl.when(not_last)
            def _():
                u_copy(i).start()

            @pl.when(not_first)
            def _():
                d_copy(CHUNKS - 1 - i).start()

            return carry

        def halo_here(step):
            @pl.when(not_first)
            def _():
                u_copy(step).wait_recv()

            @pl.when(not_last)
            def _():
                d_copy(CHUNKS - 1 - step).wait_recv()

        def table_copies(i):
            return [
                pltpu.make_async_remote_copy(
                    ref.at[tp], ref.at[tp], table_send.at[j, i], table_recv.at[j, i],
                    device_id=z_peers[i], device_id_type=MESH,
                )
                for j, ref in enumerate((table, groups))
            ]

        @pl.when(ctx == 0)
        def _():
            u_in[...] = jnp.zeros_like(u_in)

        @pl.when(ctx == ctx_size - 1)
        def _():
            d_in[...] = jnp.zeros_like(d_in)

        for p in range(pieces):
            edge_copy(0, p).wait()
            edge_copy(1, p).wait()
            ch, ln = edge_rows(0, p), pl.ds(positions - TAPS, TAPS)
            u_out[:, ch, :] = k[:, ch, ln] * v[:, ch, ln]
            edge_copy(2, p).wait()
            edge_copy(3, p).wait()
            ch, ln = edge_rows(2, p), pl.ds(0, TAPS)
            d_out[:, ch, :] = q[:, ch, ln] * g[:, ch, ln]
            if p == 0:
                pl.semaphore_wait(barrier, len(greeted))
            lax.fori_loop(EDGES[p], EDGES[p + 1], start_halo, 0)
            if p == 0:
                table[tp] = filt_ref[...].astype(BF16)
                groups[tp] = grp_ref[...]
                for i in range(tp_size - 1):
                    for copy in table_copies(i):
                        copy.start()
                pass_on(0, [after, before, other])
            if p == 1:
                lax.fori_loop(0, CHUNKS // 2, start_rest, 0)

        row = lax.broadcasted_iota(jnp.int32, (TAPS, TAPS), 0)
        lane = lax.broadcasted_iota(jnp.int32, (TAPS, TAPS), 1)
        masks[0] = jnp.where(lane >= row, 1.0, 0.0).astype(BF16)
        masks[1] = jnp.where(lane < row, 1.0, 0.0).astype(BF16)

        nothing = jnp.zeros((stack, TAPS), BF16)

        def run_rows(ref, r, b):
            return jnp.concatenate(
                [ref[w, aligned(r, MEMBERS), TAPS * b : TAPS * b + TAPS] for w in range(windows)], axis=0
            )

        def product(left, right, r):
            return [run_rows(left, r, b) * run_rows(right, r, b) for b in range(blocks)]

        def put(out, gate, r, value):
            for b in range(blocks):
                for w in range(windows):
                    at = (w, aligned(r, MEMBERS), slice(TAPS * b, TAPS * b + TAPS))
                    first = b * stack + w * MEMBERS
                    out[at] = (gate[at].astype(F32) * value[first : first + MEMBERS]).astype(BF16)

        def circulant(r):
            rows = jnp.broadcast_to(taps_of[pl.ds(r, 1), :], (TAPS, TAPS))
            return pltpu.roll(rows, 0, 1, stride=1, stride_axis=0).astype(BF16)

        def outer(u_four, d_four, r):
            left = jnp.concatenate(u_four, axis=0)
            shifted = [nothing] + d_four
            right = jnp.concatenate(
                [jnp.concatenate([shifted[i + 1], shifted[i]], axis=1) for i in range(blocks + 1)], axis=0
            )
            pairs = lax.dot_general(left, right, (((0,), (0,)), ((), ())), preferred_element_type=F32)
            folded = jnp.where(lane >= row, pairs[:, TAPS:], pairs[:, :TAPS])
            total = folded[0:8]
            for i in range(1, TAPS // 8):
                total = total + pltpu.roll(folded[8 * i : 8 * i + 8], TAPS - 8 * i, 1)
            partial[aligned(r, 8), :] = total

        def forward(r):
            circ = circulant(r)
            u_four = [run_rows(u_in, r, 0)] + product(k, v, r)
            weights = jnp.concatenate([circ * masks[1], circ * masks[0]], axis=0)
            left = jnp.concatenate(
                [jnp.concatenate([u_four[b], u_four[b + 1]], axis=1) for b in range(blocks)], axis=0
            )
            mixed = jnp.dot(left, weights, preferred_element_type=F32)
            put(gated, q, r, mixed)
            put(gradq, g, r, mixed)

        def backward(r):
            circ = circulant(r)
            d_four = product(g, q, r) + [run_rows(d_in, r, 0)]
            weights = jnp.concatenate([circ * masks[0], circ * masks[1]], axis=1)
            left = jnp.concatenate(
                [jnp.concatenate([d_four[b], d_four[b + 1]], axis=1) for b in range(blocks)], axis=0
            )
            upward = lax.dot_general(left, weights, (((1,), (1,)), ((), ())), preferred_element_type=F32)
            put(gradk, v, r, upward)
            put(gradv, k, r, upward)

        unroll = 4

        def first_phase(step, carry):
            back = CHUNKS - 1 - step
            for a in range(4):
                rest_copy(a, step).wait()
                rest_copy(a, back).wait()
            halo_here(step)

            def some(i, inner):
                for j in range(unroll):
                    r = step * chunk_runs + i * unroll + j
                    outer([run_rows(u_in, r, 0)] + product(k, v, r), product(g, q, r) + [nothing], r)
                    r = back * chunk_runs + i * unroll + j
                    outer([nothing] + product(k, v, r), product(g, q, r) + [run_rows(d_in, r, 0)], r)
                return inner

            lax.fori_loop(0, chunk_runs // unroll, some, 0)
            for c in (step, back):
                first = pl.multiple_of(c * chunk_runs * 8, chunk_runs * 8)
                total = partial[pl.ds(first, chunk_runs, stride=8), :]
                for s in range(1, 8):
                    total = total + pltpu.roll(partial[pl.ds(first + s, chunk_runs, stride=8), :], TAPS - s, 1)
                local[aligned(c, chunk_runs), :] = total
            return carry

        middle = CHUNKS // 2
        lax.fori_loop(0, EARLY, first_phase, 0)

        pl.semaphore_wait(known.at[0], 3)
        pass_on(1, [along(2), along(-2)])
        for i in range(tp_size - 1):
            for copy in table_copies(i):
                copy.wait()

        def run_groups(z):
            ids = groups[z]
            span = TAPS // MEMBERS
            pick = jnp.where(
                lax.broadcasted_iota(jnp.int32, (runs, channels // TAPS), 1)
                == lax.broadcasted_iota(jnp.int32, (runs, channels // TAPS), 0) // span,
                1.0, 0.0,
            ).astype(BF16)
            high = jnp.dot(pick, (ids >> 4).astype(F32).astype(BF16), preferred_element_type=F32)
            low = jnp.dot(pick, (ids & 15).astype(F32).astype(BF16), preferred_element_type=F32)
            r = lax.broadcasted_iota(jnp.int32, (runs, TAPS), 0)
            l = lax.broadcasted_iota(jnp.int32, (runs, TAPS), 1)
            keep = jnp.where(l == (r % span) * MEMBERS, high * 16.0 + low, 0.0)
            return jnp.sum(keep, axis=1, keepdims=True)

        mine = run_groups(tp)
        rows_here = GROUPS // tp_size
        chosen = jnp.zeros((runs, TAPS), F32)
        for z in range(tp_size):
            ids = lax.broadcasted_iota(jnp.int32, (runs, rows_here), 1) + z * rows_here
            onehot = jnp.where(ids.astype(F32) == mine, 1.0, 0.0).astype(BF16)
            chosen = chosen + jnp.dot(onehot, table[z], preferred_element_type=F32)
        taps_of[...] = chosen
        first_row = tp * rows_here
        for z in range(tp_size):
            ids = lax.broadcasted_iota(jnp.int32, (runs, rows_here), 1) + first_row
            onehot = jnp.where(ids.astype(F32) == run_groups(z), 1.0, 0.0)
            routes[:, runs * z : runs * (z + 1)] = onehot.T.astype(BF16)

        lax.fori_loop(EARLY, LATER, first_phase, 0)
        pl.semaphore_wait(known.at[1], 2)
        pass_on(2, [along(4), along(-4)])
        lax.fori_loop(LATER, middle, first_phase, 0)
        pl.semaphore_wait(known.at[2], 2)

        def second_phase(step, carry):
            back = CHUNKS - 1 - step

            @pl.when(step >= middle)
            def _():
                halo_here(step)

            def some(i, inner):
                for j in range(unroll):
                    forward(step * chunk_runs + i * unroll + j)
                    backward(back * chunk_runs + i * unroll + j)
                return inner

            return lax.fori_loop(0, chunk_runs // unroll, some, carry)

        own = aligned(dp, half)
        theirs = aligned(1 - dp, half)
        core_copy = pltpu.make_async_remote_copy(
            local.at[theirs], core_in, core_send, core_recv, device_id=other, device_id_type=MESH
        )
        core_copy.start()
        def finish(i, carry):
            @pl.when(not_last)
            def _():
                u_copy(i).wait_send()

            @pl.when(not_first)
            def _():
                d_copy(i).wait_send()

            return carry

        lax.fori_loop(0, STEPS[0], second_phase, 0)

        def spread(ref, slot, send, recv, to):
            copies = [
                pltpu.make_async_remote_copy(
                    ref.at[slot], ref.at[slot], send.at[i], recv.at[i], device_id=peer, device_id_type=MESH
                )
                for i, peer in enumerate(to)
            ]
            for copy in copies:
                copy.start()
            return copies

        def summed(ref, count):
            result = ref[0]
            for i in range(1, count):
                result = result + ref[i]
            return result

        core_copy.wait()
        z_all[tp, dp] = local[own, :] + core_in[...]
        z_copies = spread(z_all, (tp, dp), z_send, z_recv, last_peers)
        lax.fori_loop(STEPS[0], STEPS[1], second_phase, 0)
        for copy in z_copies:
            copy.wait()
        rest = jnp.concatenate([z_all[z, core] for z in range(tp_size) for core in range(2)], axis=0)
        result = jnp.zeros((rows_here, TAPS), F32)
        for _ in range(3):
            piece_of = rest.astype(BF16)
            rest = rest - piece_of.astype(F32)
            result = result + jnp.dot(routes[...], piece_of, preferred_element_type=F32)
        routed[...] = result * scale_by
        x_all[x] = routed[own, :]
        x_copies = spread(x_all, x, x_send, x_recv, x_peers)
        lax.fori_loop(STEPS[1], CHUNKS, second_phase, 0)
        for copy in x_copies:
            copy.wait()
        y_all[y] = summed(x_all, nx)
        y_copies = spread(y_all, y, y_send, y_recv, y_peers)
        lax.fori_loop(0, CHUNKS, finish, 0)
        for copy in y_copies:
            copy.wait()
        both[dp] = summed(y_all, ny)
        last_copy = pltpu.make_async_remote_copy(
            both.at[dp], both.at[dp], last_send, last_recv, device_id=other, device_id_type=MESH
        )
        last_copy.start()
        last_copy.wait()
        gradf[: rows_here // 2, :] = both[0]
        gradf[rows_here // 2 :, :] = both[1]


    resident = pl.BlockSpec(memory_space=pltpu.VMEM)
    remote = pl.BlockSpec(memory_space=pltpu.HBM)
    big = (windows, channels, positions)
    halo = (windows, channels, TAPS)
    dma = pltpu.SemaphoreType.DMA
    results = pl.pallas_call(
        body,
        out_shape=[pltpu.VMEM(big, BF16)] * 4 + [pltpu.VMEM((GROUPS // tp_size, TAPS), F32)],
        in_specs=[resident, resident] + [remote] * 4,
        out_specs=[resident] * 5,
        scratch_shapes=[pltpu.VMEM(big, BF16)] * 4
        + [pltpu.VMEM(halo, BF16)] * 4
        + [
            pltpu.VMEM((2, TAPS, TAPS), BF16),
            pltpu.VMEM((tp_size, GROUPS // tp_size, TAPS), BF16),
            pltpu.VMEM((tp_size, channels // TAPS, TAPS), jnp.int32),
            pltpu.VMEM((runs, TAPS), F32),
            pltpu.VMEM((GROUPS // tp_size, GROUPS), BF16),
            pltpu.VMEM((runs * 8, TAPS), F32),
            pltpu.VMEM((runs, TAPS), F32),
            pltpu.VMEM((half, TAPS), F32),
            pltpu.VMEM((ny, half, TAPS), F32),
            pltpu.VMEM((nx, half, TAPS), F32),
            pltpu.VMEM((tp_size, 2, half, TAPS), F32),
            pltpu.VMEM((GROUPS // tp_size, TAPS), F32),
            pltpu.VMEM((2, GROUPS // tp_size // 2, TAPS), F32),
            dma((4, 4)), dma((4, CHUNKS)), dma((2, CHUNKS)), dma((2, CHUNKS)), dma((2, tp_size - 1)), dma((2, tp_size - 1)),
            pltpu.SemaphoreType.REGULAR((3,)), dma, dma, dma((ny - 1,)), dma((ny - 1,)), dma((nx - 1,)), dma((nx - 1,)),
            dma((2 * tp_size - 1,)), dma((2 * tp_size - 1,)), dma, dma,
        ],
        compiler_params=pltpu.CompilerParams(collective_id=0, has_side_effects=True, vmem_limit_bytes=42 << 20),
    )(filters, group_of.reshape(channels // TAPS, TAPS), queries, key_proj, value_proj, grad_output)

    def write(*refs):
        ins, outs, sem, last = refs[:5], refs[5:10], refs[10], refs[11]
        copies = [pltpu.make_async_copy(ins[4], outs[4], last)]
        part = channels // PARTS
        for w in range(windows):
            for i in range(PARTS):
                for a in range(4):
                    at = (w, pl.ds(i * part, part))
                    copies.append(pltpu.make_async_copy(ins[a].at[at], outs[a].at[at], sem.at[a, w, i]))
        for copy in copies:
            copy.start()
        for copy in copies:
            copy.wait()

    held = [pltpu.with_memory_space_constraint(r, pltpu.VMEM) for r in results]
    return pl.pallas_call(
        write,
        out_shape=[jax.ShapeDtypeStruct(big, BF16)] * 4 + [jax.ShapeDtypeStruct((GROUPS // tp_size, TAPS), F32)],
        in_specs=[resident] * 5,
        out_specs=[remote] * 5,
        scratch_shapes=[dma((4, windows, PARTS)), dma],
        compiler_params=pltpu.CompilerParams(vmem_limit_bytes=4 << 20),
    )(*held)


def solution(mesh):
    spec = P("dp", "tp", "ctx")
    nx = 4

    def call(queries, key_proj, value_proj, grad_output, filters, group_of):
        tokens = queries.shape[0] * queries.shape[2]

        def local(*args):
            return shards(*args, tokens, nx)

        return jax.shard_map(
            local,
            mesh=mesh,
            in_specs=(spec, spec, spec, spec, P("tp", None), P("tp")),
            out_specs=(spec, spec, spec, spec, P("tp", None)),
            check_vma=False,
        )(queries, key_proj, value_proj, grad_output, filters, group_of)

    return call
```

time: 52.8 us -> 49 us (0.928)
  the two profiles are of different devices: /device:TPU:0 before, /device:TPU:1 now
where the time goes in v2:
time: 49 us; the launch traced here: 48.8 us
  Pallas kernels  48.2 us (98%)
  between operations  0.64 us (1%)
    pallas_call x1, Pallas kernels, shards(): pl.pallas_call(body, out_shape=[pltpu.VMEM(big, BF16)] * 4 + [pltpu.VMEM(...  43.5 us
    pallas_call x1, Pallas kernels, shards(): pl.pallas_call(write, out_shape=[jax.ShapeDtypeStruct(big, BF16)] * 4 + [...  4.69 us

profile of v2, /device:TPU:1, one launch (start us, length us, event | category | flops | bytes accessed | tf_op | source)
XLA Modules:
  0.0 48.8 jit_solution(6141829467783378416)
XLA Ops:
  0.6 43.5 %shard_map.101 = (bf16[2,2048,384]{2,1,0:T(8,128)(2,1)S(1)}, bf16[2,2048,384]{2,1,0:T(8,128)(2,1)S(1)}, bf16[2,2048,384]{2,1,0:T(8,128)(2,1)S(1)}, bf16[2,2048,384]{2,1,0:T(8,128)(2,1)S(1)}, f32[128,128]{1,0:T(8,128)S(1)}) custom-call(f32[128,128]{1,0:T(8,128)} %filt_ref.1, s32[16,128]{1,0:T(8,128)} %bitcast.1, bf16[2,2048,384]{2,1,0:T(8,128)(2,1)} %q_hbm.1, ...), custom_call_target="tpu_custom_call" | custom-call | tf_op jit(solution)/shard_map/pallas_call | solution.py:395
  44.1 4.7 %shard_map.102 = (bf16[2,2048,384]{2,1,0:T(8,128)(2,1)}, bf16[2,2048,384]{2,1,0:T(8,128)(2,1)}, bf16[2,2048,384]{2,1,0:T(8,128)(2,1)}, bf16[2,2048,384]{2,1,0:T(8,128)(2,1)}, f32[128,128]{1,0:T(8,128)}) custom-call(bf16[2,2048,384]{2,1,0:T(8,128)(2,1)S(1)} %get-tuple-element.10.refs_0_, bf16[2,2048,384]{2,1,0:T(8,128)(2,1)S(1)} %get-tuple-element.11.refs_1_, ...), custom_call_target="tpu_custom_call" | custom-call | tf_op jit(solution)/shard_map/pallas_call | solution.py:438

commit v3 on v2

--- a/solution.py
+++ b/solution.py
@@ -233,7 +233,7 @@
             put(gradk, v, r, upward)
             put(gradv, k, r, upward)
 
-        unroll = 4
+        unroll = 8
 
         def first_phase(step, carry):
             back = CHUNKS - 1 - step

time: 49 us -> 47.4 us (0.967)
  Pallas kernels: 48.2 us -> 46.6 us
    pallas_call x1, Pallas kernels: 43.5 us -> 41.9 us  [shards(): pl.pallas_call(body, out_shape=[pltpu.VMEM(big, BF16)] * 4 + [pltpu.VMEM(...]
where the time goes in v3:
time: 47.4 us; the launch traced here: 47.2 us
  Pallas kernels  46.6 us (98%)
  between operations  0.64 us (1%)
    pallas_call x1, Pallas kernels, shards(): pl.pallas_call(body, out_shape=[pltpu.VMEM(big, BF16)] * 4 + [pltpu.VMEM(...  41.9 us
    pallas_call x1, Pallas kernels, shards(): pl.pallas_call(write, out_shape=[jax.ShapeDtypeStruct(big, BF16)] * 4 + [...  4.69 us

profile of v3, /device:TPU:1, one launch (start us, length us, event | category | flops | bytes accessed | tf_op | source)
XLA Modules:
  0.0 47.2 jit_solution(17764100041224548237)
XLA Ops:
  0.6 41.9 %shard_map.101 = (bf16[2,2048,384]{2,1,0:T(8,128)(2,1)S(1)}, bf16[2,2048,384]{2,1,0:T(8,128)(2,1)S(1)}, bf16[2,2048,384]{2,1,0:T(8,128)(2,1)S(1)}, bf16[2,2048,384]{2,1,0:T(8,128)(2,1)S(1)}, f32[128,128]{1,0:T(8,128)S(1)}) custom-call(f32[128,128]{1,0:T(8,128)} %filt_ref.1, s32[16,128]{1,0:T(8,128)} %bitcast.1, bf16[2,2048,384]{2,1,0:T(8,128)(2,1)} %q_hbm.1, ...), custom_call_target="tpu_custom_call" | custom-call | tf_op jit(solution)/shard_map/pallas_call | solution.py:395
  42.5 4.7 %shard_map.102 = (bf16[2,2048,384]{2,1,0:T(8,128)(2,1)}, bf16[2,2048,384]{2,1,0:T(8,128)(2,1)}, bf16[2,2048,384]{2,1,0:T(8,128)(2,1)}, bf16[2,2048,384]{2,1,0:T(8,128)(2,1)}, f32[128,128]{1,0:T(8,128)}) custom-call(bf16[2,2048,384]{2,1,0:T(8,128)(2,1)S(1)} %get-tuple-element.10.refs_0_, bf16[2,2048,384]{2,1,0:T(8,128)(2,1)S(1)} %get-tuple-element.11.refs_1_, ...), custom_call_target="tpu_custom_call" | custom-call | tf_op jit(solution)/shard_map/pallas_call | solution.py:438

commit v4 on v3

--- a/solution.py
+++ b/solution.py
@@ -14,8 +14,7 @@
 EARLY = 2
 LATER = 5
 EDGES = (0, 1, 4, 8, 16)
-PARTS = 1
-STEPS = (1, 8)
+UNROLL = (8, 8)
 MESH = pl.DeviceIdType.MESH
 
 
@@ -39,7 +38,7 @@
     def body(
         filt_ref, grp_ref, q_hbm, k_hbm, v_hbm, g_hbm,
         gated, gradq, gradk, gradv, gradf,
-        q, k, v, g, u_out, d_out, u_in, d_in, masks, table, groups, taps_of, routes,
+        q, k, v, g, u_out, d_out, u_in, d_in, circs, masks, table, groups, taps_of, routes,
         partial, local, core_in, y_all, x_all, z_all, routed, both,
         edge_sem, rest_sem, halo_send, halo_recv, table_send, table_recv,
         known, core_send, core_recv, y_send, y_recv, x_send, x_recv, z_send, z_recv, last_send, last_recv,
@@ -196,7 +195,9 @@
 
         def circulant(r):
             rows = jnp.broadcast_to(taps_of[pl.ds(r, 1), :], (TAPS, TAPS))
-            return pltpu.roll(rows, 0, 1, stride=1, stride_axis=0).astype(BF16)
+            made = pltpu.roll(rows, 0, 1, stride=1, stride_axis=0).astype(BF16)
+            circs[r] = made
+            return made
 
         def outer(u_four, d_four, r):
             left = jnp.concatenate(u_four, axis=0)
@@ -211,8 +212,7 @@
                 total = total + pltpu.roll(folded[8 * i : 8 * i + 8], TAPS - 8 * i, 1)
             partial[aligned(r, 8), :] = total
 
-        def forward(r):
-            circ = circulant(r)
+        def forward(r, circ):
             u_four = [run_rows(u_in, r, 0)] + product(k, v, r)
             weights = jnp.concatenate([circ * masks[1], circ * masks[0]], axis=0)
             left = jnp.concatenate(
@@ -222,8 +222,7 @@
             put(gated, q, r, mixed)
             put(gradq, g, r, mixed)
 
-        def backward(r):
-            circ = circulant(r)
+        def backward(r, circ):
             d_four = product(g, q, r) + [run_rows(d_in, r, 0)]
             weights = jnp.concatenate([circ * masks[0], circ * masks[1]], axis=1)
             left = jnp.concatenate(
@@ -233,9 +232,7 @@
             put(gradk, v, r, upward)
             put(gradv, k, r, upward)
 
-        unroll = 8
-
-        def first_phase(step, carry):
+        def gradient(step, also):
             back = CHUNKS - 1 - step
             for a in range(4):
                 rest_copy(a, step).wait()
@@ -243,24 +240,56 @@
             halo_here(step)
 
             def some(i, inner):
-                for j in range(unroll):
-                    r = step * chunk_runs + i * unroll + j
+                for j in range(UNROLL[0]):
+                    r = step * chunk_runs + i * UNROLL[0] + j
                     outer([run_rows(u_in, r, 0)] + product(k, v, r), product(g, q, r) + [nothing], r)
-                    r = back * chunk_runs + i * unroll + j
+                    if also:
+                        forward(r, circulant(r))
+                    r = back * chunk_runs + i * UNROLL[0] + j
                     outer([nothing] + product(k, v, r), product(g, q, r) + [run_rows(d_in, r, 0)], r)
+                    if also:
+                        backward(r, circulant(r))
                 return inner
 
-            lax.fori_loop(0, chunk_runs // unroll, some, 0)
+            lax.fori_loop(0, chunk_runs // UNROLL[0], some, 0)
             for c in (step, back):
                 first = pl.multiple_of(c * chunk_runs * 8, chunk_runs * 8)
                 total = partial[pl.ds(first, chunk_runs, stride=8), :]
                 for s in range(1, 8):
                     total = total + pltpu.roll(partial[pl.ds(first + s, chunk_runs, stride=8), :], TAPS - s, 1)
                 local[aligned(c, chunk_runs), :] = total
+
+        def gradient_alone(step, carry):
+            gradient(step, False)
             return carry
 
+        def gradient_and_more(step, carry):
+            gradient(step, True)
+            return carry
+
         middle = CHUNKS // 2
-        lax.fori_loop(0, EARLY, first_phase, 0)
+
+        def convolve(step, carry, made):
+            back = CHUNKS - 1 - step
+
+            def some(i, inner):
+                for j in range(UNROLL[1]):
+                    r = step * chunk_runs + i * UNROLL[1] + j
+                    forward(r, circs[r] if made else circulant(r))
+                    r = back * chunk_runs + i * UNROLL[1] + j
+                    backward(r, circs[r] if made else circulant(r))
+                return inner
+
+            return lax.fori_loop(0, chunk_runs // UNROLL[1], some, carry)
+
+        def left_over(step, carry):
+            return convolve(step, carry, False)
+
+        def second_phase(step, carry):
+            halo_here(step)
+            return convolve(step, carry, True)
+
+        lax.fori_loop(0, EARLY, gradient_alone, 0)
 
         pl.semaphore_wait(known.at[0], 3)
         pass_on(1, [along(2), along(-2)])
@@ -297,27 +326,11 @@
             onehot = jnp.where(ids.astype(F32) == run_groups(z), 1.0, 0.0)
             routes[:, runs * z : runs * (z + 1)] = onehot.T.astype(BF16)
 
-        lax.fori_loop(EARLY, LATER, first_phase, 0)
+        lax.fori_loop(EARLY, LATER, gradient_and_more, 0)
         pl.semaphore_wait(known.at[1], 2)
         pass_on(2, [along(4), along(-4)])
-        lax.fori_loop(LATER, middle, first_phase, 0)
+        lax.fori_loop(LATER, middle, gradient_alone, 0)
         pl.semaphore_wait(known.at[2], 2)
-
-        def second_phase(step, carry):
-            back = CHUNKS - 1 - step
-
-            @pl.when(step >= middle)
-            def _():
-                halo_here(step)
-
-            def some(i, inner):
-                for j in range(unroll):
-                    forward(step * chunk_runs + i * unroll + j)
-                    backward(back * chunk_runs + i * unroll + j)
-                return inner
-
-            return lax.fori_loop(0, chunk_runs // unroll, some, carry)
-
         own = aligned(dp, half)
         theirs = aligned(1 - dp, half)
         core_copy = pltpu.make_async_remote_copy(
@@ -335,7 +348,7 @@
 
             return carry
 
-        lax.fori_loop(0, STEPS[0], second_phase, 0)
+        lax.fori_loop(0, EARLY, left_over, 0)
 
         def spread(ref, slot, send, recv, to):
             copies = [
@@ -357,7 +370,7 @@
         core_copy.wait()
         z_all[tp, dp] = local[own, :] + core_in[...]
         z_copies = spread(z_all, (tp, dp), z_send, z_recv, last_peers)
-        lax.fori_loop(STEPS[0], STEPS[1], second_phase, 0)
+        lax.fori_loop(LATER, middle, left_over, 0)
         for copy in z_copies:
             copy.wait()
         rest = jnp.concatenate([z_all[z, core] for z in range(tp_size) for core in range(2)], axis=0)
@@ -369,7 +382,7 @@
         routed[...] = result * scale_by
         x_all[x] = routed[own, :]
         x_copies = spread(x_all, x, x_send, x_recv, x_peers)
-        lax.fori_loop(STEPS[1], CHUNKS, second_phase, 0)
+        lax.fori_loop(middle, CHUNKS, second_phase, 0)
         for copy in x_copies:
             copy.wait()
         y_all[y] = summed(x_all, nx)
@@ -400,6 +413,7 @@
         scratch_shapes=[pltpu.VMEM(big, BF16)] * 4
         + [pltpu.VMEM(halo, BF16)] * 4
         + [
+            pltpu.VMEM((runs, TAPS, TAPS), BF16),
             pltpu.VMEM((2, TAPS, TAPS), BF16),
             pltpu.VMEM((tp_size, GROUPS // tp_size, TAPS), BF16),
             pltpu.VMEM((tp_size, channels // TAPS, TAPS), jnp.int32),
@@ -423,12 +437,7 @@
     def write(*refs):
         ins, outs, sem, last = refs[:5], refs[5:10], refs[10], refs[11]
         copies = [pltpu.make_async_copy(ins[4], outs[4], last)]
-        part = channels // PARTS
-        for w in range(windows):
-            for i in range(PARTS):
-                for a in range(4):
-                    at = (w, pl.ds(i * part, part))
-                    copies.append(pltpu.make_async_copy(ins[a].at[at], outs[a].at[at], sem.at[a, w, i]))
+        copies += [pltpu.make_async_copy(ins[a], outs[a], sem.at[a]) for a in range(4)]
         for copy in copies:
             copy.start()
         for copy in copies:
@@ -440,7 +449,7 @@
         out_shape=[jax.ShapeDtypeStruct(big, BF16)] * 4 + [jax.ShapeDtypeStruct((GROUPS // tp_size, TAPS), F32)],
         in_specs=[resident] * 5,
         out_specs=[remote] * 5,
-        scratch_shapes=[dma((4, windows, PARTS)), dma],
+        scratch_shapes=[dma((4,)), dma],
         compiler_params=pltpu.CompilerParams(vmem_limit_bytes=4 << 20),
     )(*held)
 

time: 47.4 us -> 47.4 us (level)
  no operation moved by 1% of the time
where the time goes in v4:
time: 47.4 us; the launch traced here: 47.3 us
  Pallas kernels  46.6 us (98%)
  between operations  0.64 us (1%)
    pallas_call x1, Pallas kernels, shards(): pl.pallas_call(body, out_shape=[pltpu.VMEM(big, BF16)] * 4 + [pltpu.VMEM(...  41.9 us
    pallas_call x1, Pallas kernels, shards(): pl.pallas_call(write, out_shape=[jax.ShapeDtypeStruct(big, BF16)] * 4 + [...  4.75 us

profile of v4, /device:TPU:1, one launch (start us, length us, event | category | flops | bytes accessed | tf_op | source)
XLA Modules:
  0.0 47.3 jit_solution(7422561543554537501)
XLA Ops:
  0.6 41.9 %shard_map.101 = (bf16[2,2048,384]{2,1,0:T(8,128)(2,1)S(1)}, bf16[2,2048,384]{2,1,0:T(8,128)(2,1)S(1)}, bf16[2,2048,384]{2,1,0:T(8,128)(2,1)S(1)}, bf16[2,2048,384]{2,1,0:T(8,128)(2,1)S(1)}, f32[128,128]{1,0:T(8,128)S(1)}) custom-call(f32[128,128]{1,0:T(8,128)} %filt_ref.1, s32[16,128]{1,0:T(8,128)} %bitcast.1, bf16[2,2048,384]{2,1,0:T(8,128)(2,1)} %q_hbm.1, ...), custom_call_target="tpu_custom_call" | custom-call | tf_op jit(solution)/shard_map/pallas_call | solution.py:408
  42.5 4.7 %shard_map.102 = (bf16[2,2048,384]{2,1,0:T(8,128)(2,1)}, bf16[2,2048,384]{2,1,0:T(8,128)(2,1)}, bf16[2,2048,384]{2,1,0:T(8,128)(2,1)}, bf16[2,2048,384]{2,1,0:T(8,128)(2,1)}, f32[128,128]{1,0:T(8,128)}) custom-call(bf16[2,2048,384]{2,1,0:T(8,128)(2,1)S(1)} %get-tuple-element.10.refs_0_, bf16[2,2048,384]{2,1,0:T(8,128)(2,1)S(1)} %get-tuple-element.11.refs_1_, ...), custom_call_target="tpu_custom_call" | custom-call | tf_op jit(solution)/shard_map/pallas_call | solution.py:447
